TPU v7x, 512 devices: a whole 4x8x8 slice. The times are simulated.
512 devices in a mesh: ctx: 32 (over z, x), exp: 16 (over y, core).
Axes of the slice: x: 4, y: 8, z: 8, core: 2. Of those that a mesh axis runs over, the one named last changes fastest.
Arguments:
- x_ssd: bfloat16 [65536, 4096], P('ctx', 'exp'), may hold values from -6 to 6
- dt_raw: float32 [65536, 64], P('ctx', 'exp'), may hold values from -9 to -3
- a_log: float32 [64], P('exp')
- b_in: bfloat16 [65536, 1024], P('ctx', 'exp'), may hold values from -6 to 6
- c_in: bfloat16 [65536, 1024], P('ctx', 'exp'), may hold values from -0.5390625 to 0.5390625
- d_skip: float32 [64], P('exp'), may hold values from 0.1 to 2.5
- dy_ssd: bfloat16 [65536, 4096], P('ctx', 'exp'), may hold values from -6 to 6
Outputs:
- input_gradient: bfloat16 [65536, 4096], P('ctx', 'exp')
- grad_dt: float32 [65536, 64], P('ctx', 'exp')
- sensitivity_loga: float32 [64], P('exp')
- grad_b: bfloat16 [65536, 1024], P('ctx', 'exp')
- grad_c: bfloat16 [65536, 1024], P('ctx', 'exp')
- grad_dskip: float32 [64], P('exp')
All inputs are finite; a program needn't handle non-finite values.
Results may differ from a plain program's by a relative error of at most 0.00105.
Values may be sent and summed in bfloat16 or wider, within the bound.
No kernel may reach another device: no remote copies, remote signals or barrier semaphores. Data moves between devices by JAX's collectives and lax.ppermute only.
A program may use at most 128 MiB of HBM per device.

v0:
```python
import jax
import jax.numpy as jnp
from jax import lax
from jax.sharding import PartitionSpec as P

BLOCK = 128


precise = lax.Precision.HIGHEST


def from_partner(block, axis, distance):
    count = lax.axis_size(axis)
    route = []
    for low in range(count):
        high = low | 1 << distance
        if high != low and high < count:
            route += [(low, high), (high, low)]
    return lax.ppermute(block, axis, route)


def passed_along(value, axis, steps):
    count = lax.axis_size(axis)
    initial, last = (max(0, -steps), min(count, count - steps))
    return lax.ppermute(value, axis, [(source, source + steps) for source in range(initial, last)])


def ssd_forward(
    values_in, dt_values, log_decay, b_values, c_values, skip_weight, start_state, block_len
):
    length, head_count = dt_values.shape
    groups = b_values.shape[1]
    head_width = values_in.shape[1] // head_count
    values = values_in.reshape(length, head_count, head_width)
    step_size = jax.nn.softplus(dt_values)
    log_rate = -jnp.exp(log_decay)[None, :] * step_size
    b_heads = jnp.repeat(b_values, head_count // groups, axis=1)
    c_heads = jnp.repeat(c_values, head_count // groups, axis=1)
    blocks = length // block_len
    lower_mask = (jnp.arange(block_len)[:, None] >= jnp.arange(block_len)[None, :])[:, :, None]

    def blocked(array_in):
        return array_in.reshape((blocks, block_len) + array_in.shape[1:])

    def advance(carry_state, pieces):
        block_values, block_steps, block_rates, block_b, block_c = pieces
        cumulative = jnp.cumsum(block_rates, axis=0)
        spread = jnp.where(lower_mask, cumulative[:, None, :] - cumulative[None, :, :], 0.0)
        decay_lookup = jnp.where(lower_mask, jnp.exp(spread), 0.0)
        scores = jnp.einsum("thn,shn->tsh", block_c, block_b, precision=precise)
        inputs = block_steps[:, :, None] * block_values
        inner_part = jnp.einsum("tsh,shp->thp", decay_lookup * scores, inputs, precision=precise)
        carried = jnp.exp(cumulative)[:, :, None] * jnp.einsum(
            "thn,hpn->thp", block_c, carry_state, precision=precise
        )
        block_out = inner_part + carried + skip_weight[None, :, None] * block_values
        tail_decay = jnp.exp(cumulative[-1][None, :] - cumulative)
        following = jnp.exp(cumulative[-1])[:, None, None] * carry_state + jnp.einsum(
            "sh,shp,shn->hpn", tail_decay, inputs, block_b, precision=precise
        )
        return (following, block_out)

    final_state, outputs = lax.scan(
        jax.checkpoint(advance),
        start_state,
        (
            blocked(values),
            blocked(step_size),
            blocked(log_rate),
            blocked(b_heads),
            blocked(c_heads),
        ),
    )
    return (outputs.reshape(length, head_count * head_width), final_state)


def per_device(x_ssd, dt_raw, a_log, b_in, c_in, d_skip, dy_ssd):
    partner_b, partner_c = from_partner((b_in, c_in), "exp", 0)
    is_lower = lax.axis_index("exp") % 2 == 0

    def join_halves(mine, other):
        return jnp.where(
            is_lower, jnp.concatenate([mine, other], axis=1), jnp.concatenate([other, mine], axis=1)
        )

    b_full = join_halves(b_in, partner_b).astype(jnp.float32)[:, None, :]
    c_full = join_halves(c_in, partner_c).astype(jnp.float32)[:, None, :]
    length, head_count = dt_raw.shape
    head_width = x_ssd.shape[1] // head_count
    values = x_ssd.astype(jnp.float32).reshape(length, head_count, head_width)
    step_size = jax.nn.softplus(dt_raw)
    log_rate = -jnp.exp(a_log)[None, :] * step_size
    cumulative = jnp.cumsum(log_rate, axis=0)
    shard_decay = jnp.exp(cumulative[-1])
    b_vals = b_full[:, 0, :]
    c_vals = c_full[:, 0, :]
    tail_weight = jnp.exp(cumulative[-1][None, :] - cumulative) * step_size
    end_local = jnp.einsum("th,thp,tn->hpn", tail_weight, values, b_vals, precision=precise)
    upstream = dy_ssd.astype(jnp.float32).reshape(length, head_count, head_width)
    start_local = jnp.einsum(
        "th,thp,tn->hpn", jnp.exp(cumulative), upstream, c_vals, precision=precise
    )
    zero_state = jnp.zeros_like(end_local)

    def relay_turn(turn_index, carried):
        incoming, outgoing = carried
        sent_state = passed_along(shard_decay[:, None, None] * incoming + end_local, "ctx", 1)
        sent_adjoint = passed_along(shard_decay[:, None, None] * outgoing + start_local, "ctx", -1)
        return (sent_state, sent_adjoint)

    start_state, end_adjoint = lax.fori_loop(
        0, lax.axis_size("ctx") - 1, relay_turn, (zero_state, zero_state)
    )

    def forward(values_in, steps_in, logs_in, b_arg, c_arg, skips):
        return ssd_forward(values_in, steps_in, logs_in, b_arg, c_arg, skips, start_state, BLOCK)

    _, pullback = jax.vjp(forward, x_ssd.astype(jnp.float32), dt_raw, a_log, b_full, c_full, d_skip)
    grad_vals, grad_dt, sensitivity_loga, grad_bvals, grad_cvals, grad_dskip = pullback(
        (dy_ssd.astype(jnp.float32), end_adjoint)
    )
    sensitivity_loga, grad_dskip = lax.psum((sensitivity_loga, grad_dskip), "ctx")
    half_width = b_in.shape[1]
    grad_bfull = grad_bvals[:, 0, :]
    grad_cfull = grad_cvals[:, 0, :]
    keep_b = jnp.where(is_lower, grad_bfull[:, :half_width], grad_bfull[:, half_width:])
    give_b = jnp.where(is_lower, grad_bfull[:, half_width:], grad_bfull[:, :half_width])
    keep_c = jnp.where(is_lower, grad_cfull[:, :half_width], grad_cfull[:, half_width:])
    give_c = jnp.where(is_lower, grad_cfull[:, half_width:], grad_cfull[:, :half_width])
    back_b, back_c = from_partner((give_b, give_c), "exp", 0)
    grad_b = (keep_b + back_b).astype(jnp.bfloat16)
    grad_c = (keep_c + back_c).astype(jnp.bfloat16)
    return (grad_vals.astype(jnp.bfloat16), grad_dt, sensitivity_loga, grad_b, grad_c, grad_dskip)


def solution(mesh):
    return jax.shard_map(
        per_device,
        mesh=mesh,
        in_specs=(
            P("ctx", "exp"),
            P("ctx", "exp"),
            P("exp"),
            P("ctx", "exp"),
            P("ctx", "exp"),
            P("exp"),
            P("ctx", "exp"),
        ),
        out_specs=(
            P("ctx", "exp"),
            P("ctx", "exp"),
            P("exp"),
            P("ctx", "exp"),
            P("ctx", "exp"),
            P("exp"),
        ),
        check_vma=False,
    )
```

profile of v0, /device:TPU:272, one launch (start us, length us, event | category | flops | bytes accessed | tf_op | source)
XLA Modules:
  0.0 897.0 jit_solution(1814616454589555200)
XLA Ops:
  37.3 409.5 %while.51 = (s32[]{:T(128)}, f32[4,64,128]{2,1,0:T(8,128)S(1)}, f32[4,64,128]{2,1,0:T(8,128)S(1)}, f32[4]{0:T(128)S(1)}, f32[4,64,128]{2,1,0:T(8,128)}, /*index=5*/f32[4,64,128]{2,1,0:T(8,128)S(1)}, s32[]{:T(128)}) while((s32[]{:T(128)}, f32[4,64,128]{2,1,0:T(8,128)S(1)}, f32[4,64,128]{2,1,0:T(8,128)S(1)}, f32[4]{0:T(128)S(1)}, ...), condition=%wide.region_3.4_spmd, body=%wide.region_2.3_spmd.sunk | while | flops 131074 | bytes 1835181 | solution.py:111
  66.2 7.7 collective-permute-start.1
  79.3 7.7 collective-permute-start.1
  92.5 7.7 collective-permute-start.1
  105.6 7.7 collective-permute-start.1
  118.7 7.7 collective-permute-start.1
  131.8 7.7 collective-permute-start.1
  158.0 7.7 collective-permute-start.1
  171.9 7.7 collective-permute-start.1
  185.9 7.7 collective-permute-start.1
  199.0 7.7 collective-permute-start.1
  212.2 7.7 collective-permute-start.1
  238.4 7.7 collective-permute-start.1
  251.5 7.7 collective-permute-start.1
  277.7 7.7 collective-permute-start.1
  290.8 7.7 collective-permute-start.1
  304.0 7.7 collective-permute-start.1
  318.0 7.7 collective-permute-start.1
  331.8 7.7 collective-permute-start.1
  344.9 7.7 collective-permute-start.1
  371.2 7.7 collective-permute-start.1
  449.4 62.2 %while.52 = (s32[]{:T(128)}, f32[4,64,128]{2,1,0:T(8,128)S(1)}, f32[16,4,64,128]{3,2,1,0:T(8,128)}, f32[16,128,4]{2,1,0:T(8,128)}, f32[16,128,4]{1,2,0:T(4,128)}...) while((s32[]{:T(128)}, f32[4,64,128]{2,1,0:T(8,128)S(1)}, ...), condition=%wide.region_6.7_spmd, body=%wide.region_4.6_spmd.sunk | while | flops 50528256 | bytes 943817 | solution.py:63
  520.5 267.0 %while.53 = (s32[]{:T(128)}, f32[4]{0:T(128)S(1)}, f32[4,64,128]{2,1,0:T(8,128)S(1)}, bf16[16,128,4,64]{1,3,2,0:T(8,128)(2,1)S(1)}, f32[16,128,4]{1,2,0:T(4,128)...) while((s32[]{:T(128)}, f32[4]{0:T(128)S(1)}, ...), condition=%wide.region_17.18_spmd.clone, body=%wide.region_7.17_spmd.clone.sunk | while | flops 656657920 | bytes 10521631 | solution.py:63
  807.2 75.9 %all-reduce.2 = (f32[4]{0:T(128)}, f32[4]{0:T(128)}) all-reduce(f32[4]{0:T(128)S(1)} %negate_multiply_fusion, f32[4]{0:T(128)S(1)} %get-tuple-element.430), channel_id=1, replica_groups=mesh['ctx'=32,'exp'=16] {'ctx'}, use_global_device_ids=true, to_apply=%region_19.20 | all-reduce | flops 8 | bytes 64 | tf_op jit(solution)/shard_map/psum | solution.py:122
  (987 shorter events, 663.2 us)
Async XLA Ops:
  0.6 26.0 %collective-permute-start.3 = (bf16[2048,64]{0,1:T(8,128)(2,1)}, bf16[2048,64]{0,1:T(8,128)(2,1)}, u32[]{:S(2)}, u32[]{:S(2)}) collective-permute-start(bf16[2048,64]{0,1:T(8,128)(2,1)} %param.17), channel_id=1, source_target_pairs={{0,1},{1,0},{2,3},{3,2},{4,5},{5,4},{6,7},{7,6},{8,9},{9,8},{10,11... | collective-permute-start | bytes 786440 | tf_op jit(solution)/shard_map/ppermute | solution.py:19
  2.7 22.0 %collective-permute-start.2 = (bf16[2048,64]{0,1:T(8,128)(2,1)}, bf16[2048,64]{0,1:T(8,128)(2,1)}, u32[]{:S(2)}, u32[]{:S(2)}) collective-permute-start(bf16[2048,64]{0,1:T(8,128)(2,1)} %param.16), channel_id=1, source_target_pairs={{0,1},{1,0},{2,3},{3,2},{4,5},{5,4},{6,7},{7,6},{8,9},{9,8},{10,11... | collective-permute-start | bytes 786440 | tf_op jit(solution)/shard_map/ppermute | solution.py:19
  38.4 10.6 %collective-permute-start = (f32[4,64,128]{2,1,0:T(8,128)S(1)}, f32[4,64,128]{2,1,0:T(8,128)S(1)}, u32[]{:S(2)}, u32[]{:S(2)}) collective-permute-start(f32[4,64,128]{2,1,0:T(8,128)S(1)} %get-tuple-element.894), channel_id=1, source_target_pairs={{0,16},{16,32},{32,48},{48,64},{64,80},{80,96},{96,112},{112,128},... | collective-permute-start | bytes 393224 | tf_op jit(solution)/shard_map/while/body/eval_jaxpr/ppermute | solution.py:25
  51.2 10.6 %collective-permute-start = (f32[4,64,128]{2,1,0:T(8,128)S(1)}, f32[4,64,128]{2,1,0:T(8,128)S(1)}, u32[]{:S(2)}, u32[]{:S(2)}) collective-permute-start(f32[4,64,128]{2,1,0:T(8,128)S(1)} %get-tuple-element.894), channel_id=1, source_target_pairs={{0,16},{16,32},{32,48},{48,64},{64,80},{80,96},{96,112},{112,128},... | collective-permute-start | bytes 393224 | tf_op jit(solution)/shard_map/while/body/eval_jaxpr/ppermute | solution.py:25
  64.3 10.6 %collective-permute-start = (f32[4,64,128]{2,1,0:T(8,128)S(1)}, f32[4,64,128]{2,1,0:T(8,128)S(1)}, u32[]{:S(2)}, u32[]{:S(2)}) collective-permute-start(f32[4,64,128]{2,1,0:T(8,128)S(1)} %get-tuple-element.894), channel_id=1, source_target_pairs={{0,16},{16,32},{32,48},{48,64},{64,80},{80,96},{96,112},{112,128},... | collective-permute-start | bytes 393224 | tf_op jit(solution)/shard_map/while/body/eval_jaxpr/ppermute | solution.py:25
  90.5 10.6 %collective-permute-start = (f32[4,64,128]{2,1,0:T(8,128)S(1)}, f32[4,64,128]{2,1,0:T(8,128)S(1)}, u32[]{:S(2)}, u32[]{:S(2)}) collective-permute-start(f32[4,64,128]{2,1,0:T(8,128)S(1)} %get-tuple-element.894), channel_id=1, source_target_pairs={{0,16},{16,32},{32,48},{48,64},{64,80},{80,96},{96,112},{112,128},... | collective-permute-start | bytes 393224 | tf_op jit(solution)/shard_map/while/body/eval_jaxpr/ppermute | solution.py:25
  103.6 10.6 %collective-permute-start = (f32[4,64,128]{2,1,0:T(8,128)S(1)}, f32[4,64,128]{2,1,0:T(8,128)S(1)}, u32[]{:S(2)}, u32[]{:S(2)}) collective-permute-start(f32[4,64,128]{2,1,0:T(8,128)S(1)} %get-tuple-element.894), channel_id=1, source_target_pairs={{0,16},{16,32},{32,48},{48,64},{64,80},{80,96},{96,112},{112,128},... | collective-permute-start | bytes 393224 | tf_op jit(solution)/shard_map/while/body/eval_jaxpr/ppermute | solution.py:25
  129.8 10.6 %collective-permute-start = (f32[4,64,128]{2,1,0:T(8,128)S(1)}, f32[4,64,128]{2,1,0:T(8,128)S(1)}, u32[]{:S(2)}, u32[]{:S(2)}) collective-permute-start(f32[4,64,128]{2,1,0:T(8,128)S(1)} %get-tuple-element.894), channel_id=1, source_target_pairs={{0,16},{16,32},{32,48},{48,64},{64,80},{80,96},{96,112},{112,128},... | collective-permute-start | bytes 393224 | tf_op jit(solution)/shard_map/while/body/eval_jaxpr/ppermute | solution.py:25
  156.1 11.1 %collective-permute-start = (f32[4,64,128]{2,1,0:T(8,128)S(1)}, f32[4,64,128]{2,1,0:T(8,128)S(1)}, u32[]{:S(2)}, u32[]{:S(2)}) collective-permute-start(f32[4,64,128]{2,1,0:T(8,128)S(1)} %get-tuple-element.894), channel_id=1, source_target_pairs={{0,16},{16,32},{32,48},{48,64},{64,80},{80,96},{96,112},{112,128},... | collective-permute-start | bytes 393224 | tf_op jit(solution)/shard_map/while/body/eval_jaxpr/ppermute | solution.py:25
  158.0 11.0 %collective-permute-start.1 = (f32[4,64,128]{2,1,0:T(8,128)S(1)}, f32[4,64,128]{2,1,0:T(8,128)S(1)}, u32[]{:S(2)}, u32[]{:S(2)}) collective-permute-start(f32[4,64,128]{2,1,0:T(8,128)S(1)} %get-tuple-element.895), channel_id=1, source_target_pairs={{16,0},{32,16},{48,32},{64,48},{80,64},{96,80},{112,96},{128,112},... | collective-permute-start | bytes 393224 | tf_op jit(solution)/shard_map/while/body/eval_jaxpr/ppermute | solution.py:25
  170.0 11.8 %collective-permute-start = (f32[4,64,128]{2,1,0:T(8,128)S(1)}, f32[4,64,128]{2,1,0:T(8,128)S(1)}, u32[]{:S(2)}, u32[]{:S(2)}) collective-permute-start(f32[4,64,128]{2,1,0:T(8,128)S(1)} %get-tuple-element.894), channel_id=1, source_target_pairs={{0,16},{16,32},{32,48},{48,64},{64,80},{80,96},{96,112},{112,128},... | collective-permute-start | bytes 393224 | tf_op jit(solution)/shard_map/while/body/eval_jaxpr/ppermute | solution.py:25
  171.9 11.0 %collective-permute-start.1 = (f32[4,64,128]{2,1,0:T(8,128)S(1)}, f32[4,64,128]{2,1,0:T(8,128)S(1)}, u32[]{:S(2)}, u32[]{:S(2)}) collective-permute-start(f32[4,64,128]{2,1,0:T(8,128)S(1)} %get-tuple-element.895), channel_id=1, source_target_pairs={{16,0},{32,16},{48,32},{64,48},{80,64},{96,80},{112,96},{128,112},... | collective-permute-start | bytes 393224 | tf_op jit(solution)/shard_map/while/body/eval_jaxpr/ppermute | solution.py:25
  183.9 11.0 %collective-permute-start = (f32[4,64,128]{2,1,0:T(8,128)S(1)}, f32[4,64,128]{2,1,0:T(8,128)S(1)}, u32[]{:S(2)}, u32[]{:S(2)}) collective-permute-start(f32[4,64,128]{2,1,0:T(8,128)S(1)} %get-tuple-element.894), channel_id=1, source_target_pairs={{0,16},{16,32},{32,48},{48,64},{64,80},{80,96},{96,112},{112,128},... | collective-permute-start | bytes 393224 | tf_op jit(solution)/shard_map/while/body/eval_jaxpr/ppermute | solution.py:25
  197.1 10.6 %collective-permute-start = (f32[4,64,128]{2,1,0:T(8,128)S(1)}, f32[4,64,128]{2,1,0:T(8,128)S(1)}, u32[]{:S(2)}, u32[]{:S(2)}) collective-permute-start(f32[4,64,128]{2,1,0:T(8,128)S(1)} %get-tuple-element.894), channel_id=1, source_target_pairs={{0,16},{16,32},{32,48},{48,64},{64,80},{80,96},{96,112},{112,128},... | collective-permute-start | bytes 393224 | tf_op jit(solution)/shard_map/while/body/eval_jaxpr/ppermute | solution.py:25
  210.3 10.6 %collective-permute-start = (f32[4,64,128]{2,1,0:T(8,128)S(1)}, f32[4,64,128]{2,1,0:T(8,128)S(1)}, u32[]{:S(2)}, u32[]{:S(2)}) collective-permute-start(f32[4,64,128]{2,1,0:T(8,128)S(1)} %get-tuple-element.894), channel_id=1, source_target_pairs={{0,16},{16,32},{32,48},{48,64},{64,80},{80,96},{96,112},{112,128},... | collective-permute-start | bytes 393224 | tf_op jit(solution)/shard_map/while/body/eval_jaxpr/ppermute | solution.py:25
  223.4 10.6 %collective-permute-start = (f32[4,64,128]{2,1,0:T(8,128)S(1)}, f32[4,64,128]{2,1,0:T(8,128)S(1)}, u32[]{:S(2)}, u32[]{:S(2)}) collective-permute-start(f32[4,64,128]{2,1,0:T(8,128)S(1)} %get-tuple-element.894), channel_id=1, source_target_pairs={{0,16},{16,32},{32,48},{48,64},{64,80},{80,96},{96,112},{112,128},... | collective-permute-start | bytes 393224 | tf_op jit(solution)/shard_map/while/body/eval_jaxpr/ppermute | solution.py:25
  249.6 10.6 %collective-permute-start = (f32[4,64,128]{2,1,0:T(8,128)S(1)}, f32[4,64,128]{2,1,0:T(8,128)S(1)}, u32[]{:S(2)}, u32[]{:S(2)}) collective-permute-start(f32[4,64,128]{2,1,0:T(8,128)S(1)} %get-tuple-element.894), channel_id=1, source_target_pairs={{0,16},{16,32},{32,48},{48,64},{64,80},{80,96},{96,112},{112,128},... | collective-permute-start | bytes 393224 | tf_op jit(solution)/shard_map/while/body/eval_jaxpr/ppermute | solution.py:25
  302.0 11.2 %collective-permute-start = (f32[4,64,128]{2,1,0:T(8,128)S(1)}, f32[4,64,128]{2,1,0:T(8,128)S(1)}, u32[]{:S(2)}, u32[]{:S(2)}) collective-permute-start(f32[4,64,128]{2,1,0:T(8,128)S(1)} %get-tuple-element.894), channel_id=1, source_target_pairs={{0,16},{16,32},{32,48},{48,64},{64,80},{80,96},{96,112},{112,128},... | collective-permute-start | bytes 393224 | tf_op jit(solution)/shard_map/while/body/eval_jaxpr/ppermute | solution.py:25
  304.0 11.1 %collective-permute-start.1 = (f32[4,64,128]{2,1,0:T(8,128)S(1)}, f32[4,64,128]{2,1,0:T(8,128)S(1)}, u32[]{:S(2)}, u32[]{:S(2)}) collective-permute-start(f32[4,64,128]{2,1,0:T(8,128)S(1)} %get-tuple-element.895), channel_id=1, source_target_pairs={{16,0},{32,16},{48,32},{64,48},{80,64},{96,80},{112,96},{128,112},... | collective-permute-start | bytes 393224 | tf_op jit(solution)/shard_map/while/body/eval_jaxpr/ppermute | solution.py:25
  316.0 11.7 %collective-permute-start = (f32[4,64,128]{2,1,0:T(8,128)S(1)}, f32[4,64,128]{2,1,0:T(8,128)S(1)}, u32[]{:S(2)}, u32[]{:S(2)}) collective-permute-start(f32[4,64,128]{2,1,0:T(8,128)S(1)} %get-tuple-element.894), channel_id=1, source_target_pairs={{0,16},{16,32},{32,48},{48,64},{64,80},{80,96},{96,112},{112,128},... | collective-permute-start | bytes 393224 | tf_op jit(solution)/shard_map/while/body/eval_jaxpr/ppermute | solution.py:25
  318.0 10.9 %collective-permute-start.1 = (f32[4,64,128]{2,1,0:T(8,128)S(1)}, f32[4,64,128]{2,1,0:T(8,128)S(1)}, u32[]{:S(2)}, u32[]{:S(2)}) collective-permute-start(f32[4,64,128]{2,1,0:T(8,128)S(1)} %get-tuple-element.895), channel_id=1, source_target_pairs={{16,0},{32,16},{48,32},{64,48},{80,64},{96,80},{112,96},{128,112},... | collective-permute-start | bytes 393224 | tf_op jit(solution)/shard_map/while/body/eval_jaxpr/ppermute | solution.py:25
  329.9 10.8 %collective-permute-start = (f32[4,64,128]{2,1,0:T(8,128)S(1)}, f32[4,64,128]{2,1,0:T(8,128)S(1)}, u32[]{:S(2)}, u32[]{:S(2)}) collective-permute-start(f32[4,64,128]{2,1,0:T(8,128)S(1)} %get-tuple-element.894), channel_id=1, source_target_pairs={{0,16},{16,32},{32,48},{48,64},{64,80},{80,96},{96,112},{112,128},... | collective-permute-start | bytes 393224 | tf_op jit(solution)/shard_map/while/body/eval_jaxpr/ppermute | solution.py:25
  791.6 98.3 %collective-permute-start.5 = (f32[2048,64]{0,1:T(8,128)}, f32[2048,64]{0,1:T(8,128)}, u32[]{:S(2)}, u32[]{:S(2)}) collective-permute-start(f32[2048,64]{0,1:T(8,128)} %copy.205), channel_id=1, source_target_pairs={{0,1},{1,0},{2,3},{3,2},{4,5},{5,4},{6,7},{7,6},{8,9},{9,8},{10,11... | collective-permute-start | bytes 1572872 | tf_op jit(solution)/shard_map/ppermute | solution.py:19
  802.4 92.0 %collective-permute-start.4 = (f32[2048,64]{0,1:T(8,128)}, f32[2048,64]{0,1:T(8,128)}, u32[]{:S(2)}, u32[]{:S(2)}) collective-permute-start(f32[2048,64]{0,1:T(8,128)} %copy.203), channel_id=1, source_target_pairs={{0,1},{1,0},{2,3},{3,2},{4,5},{5,4},{6,7},{7,6},{8,9},{9,8},{10,11... | collective-permute-start | bytes 1572872 | tf_op jit(solution)/shard_map/ppermute | solution.py:19
  (52 other events, 472.7 us)
where the time goes:
time: 904 us; the launch traced here: 897 us
  starting transfers between devices  306 us (34%)
  local copies, waits for them, and re-layouts  202 us (22%)
  matrix products  148 us (16%)
  waiting for transfers between devices  80.7 us (9%)
  other arithmetic  80.1 us (9%)
  blocking collectives  75.9 us (8%)
    ppermute x62, starting transfers between devices, passed_along(): lax.ppermute(value, axis, [(source, source + steps) for source in range(i...  297 us
    squeeze x96, local copies, waits for them, and re-layouts, ssd_forward(): lax.scan(jax.checkpoint(advance), start_state, (blocked(values), blocked(...  84.7 us
    ppermute x62, waiting for transfers between devices, passed_along(): lax.ppermute(value, axis, [(source, source + steps) for source in range(i...  80.7 us
    psum x1, blocking collectives, per_device(): lax.psum((sensitivity_loga, grad_dskip), 'ctx')  75.9 us
    dot_general x48, matrix products, advance(): scores = jnp.einsum('thn,shn->tsh', block_c, block_b, precision=precise)  54.6 us
    dot_general x48, matrix products, advance(): jnp.einsum('sh,shp,shn->hpn', tail_decay, inputs, block_b, precision=prec...  41.3 us
    add x31, other arithmetic, relay_turn(): shard_decay[:, None, None] * outgoing + start_local  30.8 us
    dot_general x48, matrix products, advance(): jnp.einsum('thn,hpn->thp', block_c, carry_state, precision=precise)  25.7 us
  transfers between devices with their start and end apart: 66, of which 62 were waited for; matrix products, arithmetic and copies ran while one was open for 5% of the time, Pallas kernels for 0%

commit v1 on v0

v1 whole, which is shorter than its diff:
```python
import functools

import jax
import jax.numpy as jnp
from jax import lax
from jax.experimental import pallas as pl
from jax.experimental.pallas import tpu as pltpu
from jax.sharding import PartitionSpec as P

T = 128
F32 = jnp.float32
BF16 = jnp.bfloat16
VMEM_LIMIT = 56 * 2**20
TURNS = 2


def dot(a, b, contract=((1,), (0,)), precision=None):
    return lax.dot_general(a, b, (contract, ((), ())), precision=precision, preferred_element_type=F32)


NT = ((1,), (1,))
EXACT = lax.Precision.HIGHEST


def split(v):
    high = v.astype(BF16)
    return high, (v - high.astype(F32)).astype(BF16)


def parts(v, count):
    out = []
    for _ in range(count):
        piece = v.astype(BF16)
        out.append(piece)
        v = v - piece.astype(F32)
    return jnp.concatenate(out, axis=0)


def unit():
    i0 = lax.broadcasted_iota(jnp.int32, (T, T), 0)
    i1 = lax.broadcasted_iota(jnp.int32, (T, T), 1)
    return jnp.where(i0 == i1, 1.0, 0.0).astype(BF16)


def spread_out(rows, width):
    count = rows.shape[0]
    row = lax.broadcasted_iota(jnp.int32, (count, count * width), 0)
    lane = lax.broadcasted_iota(jnp.int32, (count, count * width), 1)
    place = jnp.where(lane // width == row, 1.0, 0.0).astype(BF16)
    return dot(parts(rows, 2), jnp.concatenate([place, place], axis=0), ((0,), (0,)))


def head_rows(heads, width):
    row = lax.broadcasted_iota(jnp.int32, (8, heads * width), 0)
    lane = lax.broadcasted_iota(jnp.int32, (8, heads * width), 1)
    return jnp.where(lane // width == row, 1.0, 0.0).astype(BF16)


def steps_kernel(heads, dt_ref, alog_ref, tab_ref, decay_ref):
    blocks = dt_ref.shape[1] // T
    rows = blocks * heads
    raw = jnp.concatenate([dt_ref[:, k * T : (k + 1) * T] for k in range(blocks)], axis=0)
    step = jnp.maximum(raw, 0.0) + jnp.log1p(jnp.exp(-jnp.abs(raw)))
    head = lax.broadcasted_iota(jnp.int32, (rows, T), 0) % heads
    scale = jnp.full((rows, T), alog_ref[0], F32)
    for h in range(1, heads):
        scale = jnp.where(head == h, alog_ref[h], scale)
    rate = -jnp.exp(scale) * step
    i0 = lax.broadcasted_iota(jnp.int32, (T, T), 0)
    i1 = lax.broadcasted_iota(jnp.int32, (T, T), 1)
    cum = dot(rate, jnp.where(i0 <= i1, 1.0, 0.0).astype(F32), precision=EXACT)
    r0 = lax.broadcasted_iota(jnp.int32, (rows, rows), 0)
    r1 = lax.broadcasted_iota(jnp.int32, (rows, rows), 1)
    same = (r0 % heads) == (r1 % heads)
    total = jnp.broadcast_to(cum[:, T - 1 : T], (rows, T))
    before = dot(jnp.where(same & (r1 // heads < r0 // heads), 1.0, 0.0).astype(F32), total, precision=EXACT)
    after = dot(jnp.where(same & (r1 // heads > r0 // heads), 1.0, 0.0).astype(F32), total, precision=EXACT)
    cum_all = before + cum
    rest = total - cum
    to_end = after + rest
    columns = [
        cum,
        step,
        step * jnp.exp(to_end),
        jnp.exp(cum_all),
        cum_all,
        to_end,
        step * jnp.exp(rest),
        jnp.exp(cum),
        jnp.log(step) - cum,
        jnp.exp(total),
    ]
    for k in range(blocks):
        for j, v in enumerate(columns):
            tab_ref[k, j * heads : (j + 1) * heads, :] = v[k * heads : (k + 1) * heads]
    decay_ref[...] = jnp.concatenate([jnp.exp((before + total)[rows - heads :, :])] * (8 // heads), axis=0)


def ends_kernel(
    heads, width, x_ref, dy_ref, b_ref, pb_ref, c_ref, pc_ref, tab_ref, decay_ref,
    msg_ref, xh_ref, xl_ref, yh_ref, yl_ref, bt_ref, ct_ref, ends, skips,
):
    step, last = pl.program_id(0), pl.num_programs(0) - 1
    ring = msg_ref.shape[0]
    full = heads * width
    state = 2 * b_ref.shape[0]
    eye = unit()

    @pl.when(step == 0)
    def _():
        ends[...] = jnp.zeros_like(ends)
        skips[...] = jnp.zeros_like(skips)

    ks = range(tab_ref.shape[0])
    at = [slice(k * T, (k + 1) * T) for k in ks]
    weights = [spread_out(tab_ref[k, 2 * heads : 4 * heads, :], width) for k in ks]
    bts = [jnp.concatenate([b_ref[:, at[k]], pb_ref[:, at[k]]], axis=0) for k in ks]
    cts = [jnp.concatenate([c_ref[:, at[k]], pc_ref[:, at[k]]], axis=0) for k in ks]
    turned = [dot(eye, jnp.concatenate([bts[k], cts[k]], axis=0), NT).astype(BF16) for k in ks]
    xw = [split(x_ref[at[k], :].astype(F32) * weights[k][:, :full]) for k in ks]
    yw = [split(dy_ref[at[k], :].astype(F32) * weights[k][:, full:]) for k in ks]
    u = ends[0] + sum(
        dot(jnp.concatenate([bts[k], bts[k]], axis=1), jnp.concatenate(xw[k], axis=0)) for k in ks
    )
    v = ends[1] + sum(
        dot(jnp.concatenate([cts[k], cts[k]], axis=1), jnp.concatenate(yw[k], axis=0)) for k in ks
    )
    skip = skips[...]
    for k in ks:
        xh_ref[at[k], :], xl_ref[at[k], :] = xw[k]
        yh_ref[at[k], :], yl_ref[at[k], :] = yw[k]
        bt_ref[at[k], :] = turned[k][:, :state]
        ct_ref[at[k], :] = turned[k][:, state:]
        skip = skip + jnp.sum((x_ref[at[k], :].astype(F32) * dy_ref[at[k], :].astype(F32)).reshape(T // 8, 8, full), axis=0)
    ends[0] = u
    ends[1] = v
    skips[...] = skip

    @pl.when(step == last)
    def _():
        part = state // ring
        total = jnp.sum(skip, axis=0, keepdims=True)
        lane = lax.broadcasted_iota(jnp.int32, (1, T), 1)
        decay = [
            jnp.where(lane < width, decay_ref[2 * i : 2 * i + 1, :], decay_ref[2 * i + 1 : 2 * i + 2, :])
            for i in range(heads // 2)
        ]
        rows = decay + [total[:, i * T : (i + 1) * T] for i in range(heads // 2)]
        extra = jnp.concatenate(rows + [jnp.zeros((8 - len(rows), T), F32)], axis=0)
        for i in range(ring):
            msg_ref[i, 0:part, 0:full] = u[i * part : (i + 1) * part]
            msg_ref[i, part : 2 * part, 0:full] = v[i * part : (i + 1) * part]
            msg_ref[i, :, full : full + 128] = extra


def relay_kernel(heads, got_ref, _, msg_ref, skip_ref):
    ring, tile, width = msg_ref.shape
    first = lax.broadcasted_iota(jnp.int32, (tile, width), 0) < tile // 2

    def decay(j):
        return jnp.concatenate([got_ref[j, i : i + 1, width : width + 128] for i in range(width // 128)], axis=1)

    state = jnp.zeros((tile, width), F32)
    skip = jnp.zeros((tile, 128), F32)
    for j in range(ring):
        msg_ref[j] = state
        state = decay(j) * state + got_ref[j, :, 0:width]
        skip = skip + got_ref[j, :, width : width + 128]
    parts = width // 128
    per = heads // parts
    row = lax.broadcasted_iota(jnp.int32, (8, 128), 0)
    lane = lax.broadcasted_iota(jnp.int32, (8, 128), 1) // (128 // per)
    out = jnp.zeros((8, 128), F32)
    for i in range(parts):
        out = jnp.where(row == i * per + lane, skip[parts + i : parts + i + 1], out)
    skip_ref[...] = out
    state = jnp.zeros((tile, width), F32)
    for j in reversed(range(ring)):
        msg_ref[j] = jnp.where(first, msg_ref[j], state)
        state = decay(j) * state + got_ref[j, :, 0:width]


def inner_kernel(heads, width, x_ref, dy_ref, b_ref, pb_ref, c_ref, pc_ref, bt_ref, tab_ref, gx_ref, gb_ref, gc_ref, read_ref):
    i0 = lax.broadcasted_iota(jnp.int32, (T, T), 0)
    i1 = lax.broadcasted_iota(jnp.int32, (T, T), 1)
    seen = i1 >= i0
    row = lax.broadcasted_iota(jnp.int32, (6 * heads, heads * T), 0) % heads
    lane = lax.broadcasted_iota(jnp.int32, (6 * heads, heads * T), 1) // T
    mine = row == lane
    ones = jnp.ones((3 * heads, T), BF16)
    ks = range(tab_ref.shape[0])
    hs = range(heads)
    at = [slice(k * T, (k + 1) * T) for k in ks]
    lanes = [slice(h * width, (h + 1) * width) for h in hs]

    def spread(k):
        source = jnp.concatenate([parts(tab_ref[k, 8 * heads : 9 * heads, :], 3), ones], axis=0)
        reader = jnp.concatenate([ones, parts(tab_ref[k, 0:heads, :], 3)], axis=0)
        reader = jnp.where(mine, jnp.concatenate([reader] * heads, axis=1).astype(F32), 0.0).astype(BF16)
        return dot(source, reader, ((0,), (0,)))

    spreads = [spread(k) for k in ks]
    bts = [jnp.concatenate([b_ref[:, at[k]], pb_ref[:, at[k]]], axis=0) for k in ks]
    cts = [jnp.concatenate([c_ref[:, at[k]], pc_ref[:, at[k]]], axis=0) for k in ks]
    scores = [dot(bt_ref[at[k], :], cts[k]) for k in ks]
    grams = [[dot(x_ref[at[k], lanes[h]], dy_ref[at[k], lanes[h]], NT) for h in hs] for k in ks]
    mixes, weights = [], []
    for k in ks:
        mixed, reads, pairs = jnp.zeros((T, T), F32), [], []
        for h in hs:
            decay = jnp.exp(jnp.where(seen, spreads[k][:, h * T : (h + 1) * T], -jnp.inf))
            term = decay * grams[k][h]
            mixed = mixed + term
            reads.append(jnp.sum(term * scores[k], axis=0, keepdims=True))
            pairs.append(jnp.concatenate(split(decay * scores[k]), axis=1))
        read_ref[k] = jnp.concatenate(reads + [jnp.zeros((8 - heads, T), F32)], axis=0)
        mixes.append(split(mixed))
        weights.append(pairs)
    for k in ks:
        for h in hs:
            dy = dy_ref[at[k], lanes[h]]
            gx_ref[at[k], lanes[h]] = dot(weights[k][h], jnp.concatenate([dy, dy], axis=0))
    for k in ks:
        mh, ml = mixes[k]
        bt, ct = bts[k], cts[k]
        gc_ref[:, at[k]] = dot(jnp.concatenate([bt, bt], axis=1), jnp.concatenate([mh, ml], axis=0))
        gb_ref[:, at[k]] = dot(jnp.concatenate([ct, ct], axis=1), jnp.concatenate([mh, ml], axis=1), NT)


def states_kernel(
    heads, width, x_ref, dy_ref, b_ref, pb_ref, c_ref, pc_ref, bt_ref, ct_ref, xd_ref, xe_ref, yd_ref, ye_ref,
    tab_ref, read_ref, dskip_ref, alog_ref, gxi_ref, gbi_ref, gci_ref,
    gx_ref, gb_ref, gc_ref, rows_ref, slope_ref, loga_ref, states, xs, held, sums,
):
    turn, half = pl.program_id(0), pl.num_programs(0) // 2
    count = tab_ref.shape[0]
    full = heads * width
    last = count * half

    def joined(own, other, at):
        return jnp.concatenate([own[:, at], other[:, at]], axis=0)

    def across(k):
        lane = lax.broadcasted_iota(jnp.int32, (1, T), 1)
        row = tab_ref[k, 9 * heads : 10 * heads, :]
        return jnp.concatenate(
            [jnp.where(lane < width, row[2 * i : 2 * i + 1], row[2 * i + 1 : 2 * i + 2]) for i in range(heads // 2)], axis=1
        )

    @pl.when(turn == 0)
    def _():
        held[...] = jnp.zeros_like(held)
        sums[...] = jnp.zeros_like(sums)

    def at(k):
        return slice(k * T, (k + 1) * T)

    @pl.when(turn < half)
    def _():
        ks = range(count)
        weights = [spread_out(tab_ref[k, 4 * heads : 7 * heads, :], width) for k in ks]
        bts = [joined(b_ref, pb_ref, at(k)) for k in ks]
        cts = [joined(c_ref, pc_ref, at(k)) for k in ks]
        bts = [jnp.concatenate([v, v], axis=1) for v in bts]
        cts = [jnp.concatenate([v, v], axis=1) for v in cts]
        pairs = [
            jnp.concatenate(split(x_ref[at(k), :].astype(F32) * weights[k][:, 2 * full :]), axis=0) for k in ks
        ]
        for k in ks:
            xs[turn * count + k] = pairs[k]
        gains = [dot(bts[k], pairs[k]) for k in ks]
        state = held[0]
        for k in ks:
            states[turn * count + k] = state
            state = across(k) * state + gains[k]
        xd = [(xd_ref[at(k), :].astype(F32) + xe_ref[at(k), :].astype(F32)) * weights[k][:, full : 2 * full] for k in ks]
        yd = [(yd_ref[at(k), :].astype(F32) + ye_ref[at(k), :].astype(F32)) * weights[k][:, 0:full] for k in ks]
        xd = [jnp.concatenate(split(v), axis=0) for v in xd]
        yd = [jnp.concatenate(split(v), axis=0) for v in yd]
        slope_x = held[1] + sum(dot(bts[k], xd[k]) for k in ks)
        slope_y = held[2] + sum(dot(cts[k], yd[k]) for k in ks)
        held[0] = state
        held[1] = slope_x
        held[2] = slope_y

        @pl.when(turn == half - 1)
        def _():
            states[last] = state
            slope_ref[0] = slope_x
            slope_ref[1] = slope_y
            held[0] = jnp.zeros_like(state)

    @pl.when(turn >= half)
    def _():
        ks = range(count)
        select = head_rows(heads, width)
        select2 = jnp.concatenate([select, select], axis=1)
        i0 = lax.broadcasted_iota(jnp.int32, (T, T), 0)
        i1 = lax.broadcasted_iota(jnp.int32, (T, T), 1)
        suffix = jnp.where(i0 >= i1, 1.0, 0.0).astype(BF16)
        lane = lax.broadcasted_iota(jnp.int32, (1, 128), 1)
        skips = jnp.concatenate(
            [jnp.where(lane < width, dskip_ref[2 * i], dskip_ref[2 * i + 1]) for i in range(heads // 2)], axis=1
        )
        last_lane = lax.broadcasted_iota(jnp.int32, (heads, T), 1) == T - 1
        base = (2 * half - 1 - turn) * count
        weights = [spread_out(tab_ref[k, 6 * heads : 8 * heads, :], width) for k in ks]
        yw = [dy_ref[at(k), :].astype(F32) * weights[k][:, full:] for k in ks]
        ys = [split(v) for v in yw]
        cts = [joined(c_ref, pc_ref, at(k)) for k in ks]
        gains = [
            dot(jnp.concatenate([cts[k], cts[k]], axis=1), jnp.concatenate([ys[k][0], ys[k][1]], axis=0)) for k in ks
        ]
        starts = [split(states[base + k]) for k in ks]
        carried = [
            dot(jnp.concatenate([ct_ref[at(k), :]] * 2, axis=1), jnp.concatenate(starts[k], axis=0)) for k in ks
        ]
        adjoint = held[0]
        ends, edges = [None] * count, [None] * count
        for k in reversed(ks):
            ends[k] = split(adjoint)
            edges[k] = jnp.sum(adjoint * states[base + k + 1], axis=0, keepdims=True)
            adjoint = across(k) * adjoint + gains[k]
        held[0] = adjoint
        for k in ks:
            sh, sl = starts[k]
            yh, yl = ys[k]
            gc_ref[:, at(k)] = gci_ref[:, at(k)] + dot(
                jnp.concatenate([sh, sh, sl], axis=1), jnp.concatenate([yh, yl, yh], axis=1), NT
            )
        returned = [
            dot(jnp.concatenate([bt_ref[at(k), :]] * 2, axis=1), jnp.concatenate(ends[k], axis=0)) for k in ks
        ]
        for k in ks:
            ah, al = ends[k]
            pair = xs[base + k]
            xh, xl = pair[0:T], pair[T:]
            gb_ref[:, at(k)] = gbi_ref[:, at(k)] + dot(
                jnp.concatenate([ah, ah, al], axis=1), jnp.concatenate([xh, xl, xh], axis=1), NT
            )
        gxs = [gxi_ref[at(k), :] + weights[k][:, :full] * returned[k] for k in ks]
        for k in ks:
            gx_ref[at(k), :] = gxs[k] + skips * dy_ref[at(k), :].astype(F32)
        pairs = [
            jnp.concatenate(
                [
                    jnp.concatenate(split(yw[k] * carried[k]), axis=1),
                    jnp.concatenate(split(x_ref[at(k), :].astype(F32) * gxs[k]), axis=1),
                ],
                axis=0,
            )
            for k in ks
        ]
        found = [dot(select2, v, NT)[0:heads] for v in pairs]
        edges = jnp.concatenate(edges + [jnp.zeros((T - count, full), F32)], axis=0)
        edges = dot(select2, jnp.concatenate(split(edges), axis=1), NT)[0:heads]
        change = [
            found[k][:, 0:T]
            + read_ref[k, 0:heads, :]
            - found[k][:, T:]
            + jnp.where(last_lane, edges[:, k : k + 1], 0.0)
            for k in ks
        ]
        change = split(jnp.concatenate(change, axis=0))
        rate = dot(jnp.concatenate(change, axis=0), suffix)
        rate = rate[0 : count * heads] + rate[count * heads :]
        loga = sums[...]
        for k in ks:
            mine = rate[k * heads : (k + 1) * heads]
            rows_ref[k, 0:heads, :] = mine
            rows_ref[k, heads:, :] = found[k][:, T:]
            loga = loga + tab_ref[k, heads : 2 * heads, :] * mine
        sums[...] = loga

        @pl.when(turn == 2 * half - 1)
        def _():
            row = lax.broadcasted_iota(jnp.int32, (heads, T), 0)
            speed = jnp.full((heads, T), alog_ref[0], F32)
            for h in range(1, heads):
                speed = jnp.where(row == h, alog_ref[h], speed)
            loga_ref[...] = jnp.concatenate([-jnp.exp(speed) * loga, jnp.zeros((8 - heads, T), F32)], axis=0)


def edge_kernel(heads, width, got_ref, msg_ref, slope_ref, loga_ref, tab_ref, start_ref, end_ref, edge_ref, sums_ref):
    ring, tile, full = got_ref.shape
    part = tile // 2
    blocks = tab_ref.shape[0]
    start = jnp.concatenate([got_ref[i, 0:part, :] for i in range(ring)], axis=0)
    end = jnp.concatenate([got_ref[i, part:, :] for i in range(ring)], axis=0)
    local_end = jnp.concatenate([msg_ref[i, 0:part, 0:full] for i in range(ring)], axis=0)
    decay = jnp.concatenate([msg_ref[0, i : i + 1, full : full + 128] for i in range(full // 128)], axis=1)
    start_ref[0], start_ref[1] = split(start)
    end_ref[0], end_ref[1] = split(end)
    both = decay * jnp.sum(end * start, axis=0, keepdims=True)
    edge_ref[...] = jnp.broadcast_to(both + jnp.sum(end * local_end, axis=0, keepdims=True), (8, full))
    total = tab_ref[blocks - 1, 4 * heads : 5 * heads, T - 1 : T]
    row = lax.broadcasted_iota(jnp.int32, (heads, full), 0)
    lane = lax.broadcasted_iota(jnp.int32, (heads, full), 1)
    cross = jnp.sum(start * slope_ref[1] + end * slope_ref[0], axis=0, keepdims=True) + jnp.zeros((heads, full), F32)
    cross = jnp.where(lane // width == row, cross + total * both, 0.0)
    sums = loga_ref[0:heads, :]
    for i in range(full // T):
        sums = sums + cross[:, i * T : (i + 1) * T]
    sums = jnp.concatenate([sums, jnp.zeros((8 - heads, T), F32)], axis=0)
    for i in range(ring):
        sums_ref[i] = sums


def give_kernel(start_ref, end_ref, xh_ref, xl_ref, yh_ref, yl_ref, gbl_ref, gcl_ref, keep_ref, give_ref):
    sh, sl, eh, el = start_ref[0], start_ref[1], end_ref[0], end_ref[1]
    s3 = jnp.concatenate([sh, sh, sl], axis=1)
    e3 = jnp.concatenate([eh, eh, el], axis=1)
    half = keep_ref.shape[0] // 2
    wide = 2 * T
    for k in range(xh_ref.shape[0] // wide):
        at = slice(k * wide, (k + 1) * wide)
        xh, xl, yh, yl = xh_ref[at, :], xl_ref[at, :], yh_ref[at, :], yl_ref[at, :]
        gc = gcl_ref[:, at] + dot(s3, jnp.concatenate([yh, yl, yh], axis=1), NT)
        gb = gbl_ref[:, at] + dot(e3, jnp.concatenate([xh, xl, xh], axis=1), NT)
        keep_ref[0:half, at] = gb[0:half]
        keep_ref[half:, at] = gc[0:half]
        give_ref[0:half, at] = gb[half:]
        give_ref[half:, at] = gc[half:]


def finish_kernel(
    heads, width, start_ref, end_ref, edge_ref, xh_ref, xl_ref, yh_ref, yl_ref, b_ref, c_ref, tab_ref, rows_ref, dt_ref,
    alog_ref, gxl_ref, gx_ref, gdt_ref, diffs,
):
    turn, last = pl.program_id(0), pl.num_programs(0) - 1
    full = heads * width
    blocks = tab_ref.shape[0]
    count = xh_ref.shape[0] // T
    s2 = start_ref[...].reshape(2 * 128, full)
    e2 = end_ref[...].reshape(2 * 128, full)
    select = head_rows(heads, width)
    select2 = jnp.concatenate([select, select], axis=1)
    ks = range(count)
    at = [slice(k * T, (k + 1) * T) for k in ks]
    carried = [dot(jnp.concatenate([c_ref[at[k], :]] * 2, axis=1), s2) for k in ks]
    returned = [dot(jnp.concatenate([b_ref[at[k], :]] * 2, axis=1), e2) for k in ks]
    weights = [spread_out(tab_ref[turn * count + k, 2 * heads : 3 * heads, :], width) for k in ks]
    ya = [split((yh_ref[at[k], :].astype(F32) + yl_ref[at[k], :].astype(F32)) * carried[k]) for k in ks]
    xb = [split((xh_ref[at[k], :].astype(F32) + xl_ref[at[k], :].astype(F32)) * returned[k]) for k in ks]
    pairs = [jnp.concatenate([jnp.concatenate(ya[k], axis=1), jnp.concatenate(xb[k], axis=1)], axis=0) for k in ks]
    found = [dot(select2, v, NT)[0:heads] for v in pairs]
    for k in ks:
        gx_ref[at[k], :] = (gxl_ref[at[k], :] + weights[k] * returned[k]).astype(BF16)
        diffs[turn * count + k, 0:heads, :] = found[k][:, :T]
        diffs[turn * count + k, heads:, :] = found[k][:, T:]

    @pl.when(turn == last)
    def _():
        rows = blocks * heads
        edge = jnp.broadcast_to(edge_ref[0:1, :], (T, full))
        edge_rows = dot(select2, jnp.concatenate(split(edge), axis=1), NT)[0:heads]

        def gathered(ref, base):
            return jnp.concatenate([ref[k, base : base + heads, :] for k in range(blocks)], axis=0)

        own = gathered(diffs, heads)
        diff = gathered(diffs, 0) - own
        i0 = lax.broadcasted_iota(jnp.int32, (T, T), 0)
        i1 = lax.broadcasted_iota(jnp.int32, (T, T), 1)
        within = dot(diff, jnp.where(i0 >= i1, 1.0, 0.0).astype(F32), precision=EXACT)
        r0 = lax.broadcasted_iota(jnp.int32, (rows, rows), 0)
        r1 = lax.broadcasted_iota(jnp.int32, (rows, rows), 1)
        later = (r0 % heads == r1 % heads) & (r1 // heads > r0 // heads)
        after = dot(
            jnp.where(later, 1.0, 0.0).astype(F32), jnp.broadcast_to(within[:, 0:1], (rows, T)), precision=EXACT
        )
        rate_grad = gathered(rows_ref, 0) + within + after + jnp.concatenate([edge_rows] * blocks, axis=0)
        step = gathered(tab_ref, heads)
        head = lax.broadcasted_iota(jnp.int32, (rows, T), 0) % heads
        scale = jnp.full((rows, T), alog_ref[0], F32)
        for h in range(1, heads):
            scale = jnp.where(head == h, alog_ref[h], scale)
        raw = jnp.concatenate([dt_ref[:, k * T : (k + 1) * T] for k in range(blocks)], axis=0)
        slope = 1.0 / (1.0 + jnp.exp(-raw))
        gdt = ((gathered(rows_ref, heads) + own) / step - jnp.exp(scale) * rate_grad) * slope
        for k in range(blocks):
            gdt_ref[:, k * T : (k + 1) * T] = gdt[k * heads : (k + 1) * heads]


def join_kernel(keep_ref, back_ref, gb_ref, gc_ref):
    half = gb_ref.shape[0]
    gb_ref[...] = (keep_ref[0:half, :] + back_ref[0:half, :]).astype(BF16)
    gc_ref[...] = (keep_ref[half:, :] + back_ref[half:, :]).astype(BF16)


def call(kernel, name, turns, ins, outs, scratch=(), flops=10**6):
    def spec(how, shape):
        if how == "s":
            return pl.BlockSpec(memory_space=pltpu.SMEM)
        if how == "a":
            return pl.BlockSpec(memory_space=pl.ANY)
        if how == "w":
            return pl.BlockSpec(shape, lambda i: (0,) * len(shape))
        dim, cuts, place = how
        block = tuple(n // cuts if d == dim else n for d, n in enumerate(shape))
        return pl.BlockSpec(block, lambda i: tuple(place(i) if d == dim else 0 for d in range(len(shape))))

    def run(*args):
        return pl.pallas_call(
            kernel,
            name=name,
            grid=(turns,),
            out_shape=tuple(shape for shape, _ in outs),
            in_specs=[spec(how, a.shape) for how, a in zip(ins, args, strict=True)],
            out_specs=tuple(spec(how, shape.shape) for shape, how in outs),
            scratch_shapes=list(scratch),
            compiler_params=pltpu.CompilerParams(vmem_limit_bytes=VMEM_LIMIT),
            cost_estimate=pl.CostEstimate(flops=flops, bytes_accessed=flops // 10, transcendentals=0),
        )(*args)

    return run


def per_device(x, dt_raw, a_log, b_in, c_in, d_skip, dy):
    pairs = [(i, i ^ 1) for i in range(lax.axis_size("exp"))]
    ring = lax.axis_size("ctx")
    tokens, full = x.shape
    heads = dt_raw.shape[1]
    width = full // heads
    half = b_in.shape[1]
    state = 2 * half
    blocks = tokens // T
    n = TURNS
    shape = jax.ShapeDtypeStruct
    b, c, dt = b_in.T, c_in.T, dt_raw.T
    pb = lax.ppermute(b, "exp", pairs)
    pc = lax.ppermute(c, "exp", pairs)
    wide = shape((tokens, full), BF16)
    wide32 = shape((tokens, full), F32)
    long = shape((state, tokens), F32)
    narrow = shape((tokens, state), BF16)
    tile = shape((8, T), F32)
    pair = shape((2, state, full), BF16)
    part = functools.partial
    rows, cols = (0, n, lambda i: i), (1, n, lambda i: i)
    tab, decay = call(
        part(steps_kernel, heads), "steps", 1, "ws", [(shape((blocks, 10 * heads, T), F32), "w"), (tile, "w")]
    )(dt, a_log)
    msg, xh, xl, yh, yl, bt, ct = call(
        part(ends_kernel, heads, width),
        "ends",
        n,
        [rows, rows, cols, cols, cols, cols, rows, "w"],
        [(shape((ring, 8, full + 128), F32), "w")] + [(wide, rows)] * 4 + [(narrow, rows)] * 2,
        [pltpu.VMEM((2, state, full), F32), pltpu.VMEM((8, full), F32)],
    )(x, dy, b, pb, c, pc, tab, decay)
    got = lax.all_to_all(msg, "ctx", 0, 0, tiled=True)
    gxi, gbi, gci, read = call(
        part(inner_kernel, heads, width),
        "inner",
        n,
        [rows, rows, cols, cols, cols, cols, rows, rows],
        [(wide32, rows), (long, cols), (long, cols), (shape((blocks, 8, T), F32), rows)],
        flops=10**10,
    )(x, dy, b, pb, c, pc, bt, tab)
    sent, skip = call(
        part(relay_kernel, heads), "relay", 1, "wa", [(shape((ring, 8, full), F32), "w"), (tile, "w")]
    )(got, read)
    carry = lax.all_to_all(sent, "ctx", 0, 0, tiled=True)
    there_and_back = lambda i: jnp.where(i < n, i, 2 * n - 1 - i)
    forth = lambda i: jnp.minimum(i, n - 1)
    back_only = lambda i: jnp.where(i < n, n - 1, 2 * n - 1 - i)
    trows, tcols = (0, n, there_and_back), (1, n, there_and_back)
    frows = (0, n, forth)
    brows, bcols = (0, n, back_only), (1, n, back_only)
    gxl, gbl, gcl, rate, slopes, loga = call(
        part(states_kernel, heads, width),
        "states",
        2 * n,
        [trows, brows, tcols, tcols, tcols, tcols, brows, brows, frows, frows, frows, frows, trows, brows, "s", "s", brows]
        + [bcols, bcols],
        [(wide32, brows), (long, bcols), (long, bcols), (shape((blocks, 2 * heads, T), F32), brows)]
        + [(shape((2, state, full), F32), "w"), (tile, "w")],
        [
            pltpu.VMEM((blocks + 1, state, full), F32),
            pltpu.VMEM((blocks, 2 * T, full), BF16),
            pltpu.VMEM((3, state, full), F32),
            pltpu.VMEM((heads, T), F32),
        ],
        flops=10**10,
    )(x, dy, b, pb, c, pc, bt, ct, xh, xl, yh, yl, tab, read, d_skip, a_log, gxi, gbi, gci)
    start, end, edge, sums = call(
        part(edge_kernel, heads, width),
        "edge",
        1,
        "wwwww",
        [(pair, "w"), (pair, "w"), (shape((8, full), F32), "w"), (shape((ring, 8, T), F32), "w")],
    )(carry, msg, slopes, loga, tab)
    loga_all = lax.all_to_all(sums, "ctx", 0, 0, tiled=True)
    keep, give = call(
        give_kernel, "give", n, ["w", "w", rows, rows, rows, rows, cols, cols], [(long, cols)] * 2, flops=10**6
    )(start, end, xh, xl, yh, yl, gbl, gcl)
    back = lax.ppermute(give, "exp", pairs)
    gx, gdt = call(
        part(finish_kernel, heads, width),
        "finish",
        n,
        ["w", "w", "w"] + [rows] * 6 + ["w", "w", "w", "s", rows],
        [(wide, rows), (shape((heads, tokens), F32), "w")],
        [pltpu.VMEM((blocks, 2 * heads, T), F32)],
        flops=10**6,
    )(start, end, edge, xh, xl, yh, yl, bt, ct, tab, rate, dt, a_log, gxl)
    out = shape((half, tokens), BF16)
    gb, gc = call(join_kernel, "join", n, [cols, cols], [(out, cols)] * 2)(keep, back)
    grad_skip = jnp.sum(skip[0:heads], axis=1)
    grad_loga = jnp.sum(loga_all[:, 0:heads, :], axis=(0, 2))
    return gx, gdt.T, grad_loga, gb.T, gc.T, grad_skip


def solution(mesh):
    return jax.shard_map(
        per_device,
        mesh=mesh,
        in_specs=(P("ctx", "exp"), P("ctx", "exp"), P("exp"), P("ctx", "exp"), P("ctx", "exp"), P("exp"), P("ctx", "exp")),
        out_specs=(P("ctx", "exp"), P("ctx", "exp"), P("exp"), P("ctx", "exp"), P("ctx", "exp"), P("exp")),
        check_vma=False,
    )
```

time: 904 us -> 97.9 us (0.11)
  the two profiles are of different devices: /device:TPU:272 before, /device:TPU:1 now
where the time goes in v1:
time: 97.9 us; the launch traced here: 97.3 us
  Pallas kernels  46.3 us (47%)
  starting transfers between devices  36.4 us (37%)
  waiting for transfers between devices  9.4 us (10%)
  local copies, waits for them, and re-layouts  3.21 us (3%)
  other arithmetic  1.28 us (1%)
    pallas_call x9, Pallas kernels, run(): pl.pallas_call(kernel, name=name, grid=(turns,), out_shape=tuple((shape f...  46.3 us
    all_to_all x1, starting transfers between devices, per_device(): loga_all = lax.all_to_all(sums, 'ctx', 0, 0, tiled=True)  9.51 us
    ppermute x1, starting transfers between devices, per_device(): pb = lax.ppermute(b, 'exp', pairs)  8.79 us
    all_to_all x1, starting transfers between devices, per_device(): got = lax.all_to_all(msg, 'ctx', 0, 0, tiled=True)  7.53 us
    all_to_all x1, waiting for transfers between devices, per_device(): got = lax.all_to_all(msg, 'ctx', 0, 0, tiled=True)  6.54 us
    all_to_all x1, starting transfers between devices, per_device(): carry = lax.all_to_all(sent, 'ctx', 0, 0, tiled=True)  5.03 us
    ppermute x1, starting transfers between devices, per_device(): back = lax.ppermute(give, 'exp', pairs)  3.61 us
    unnamed x12, local copies, waits for them, and re-layouts  3.21 us
  transfers between devices with their start and end apart: 6, of which 2 were waited for; matrix products, arithmetic and copies ran while one was open for 1% of the time, Pallas kernels for 29%

profile of v1, /device:TPU:1, one launch (start us, length us, event | category | flops | bytes accessed | tf_op | source)
XLA Modules:
  0.0 97.3 jit_solution(6526958171869309014)
XLA Ops:
  0.6 8.8 %collective-permute-start = (bf16[64,2048]{1,0:T(8,128)(2,1)}, bf16[64,2048]{1,0:T(8,128)(2,1)S(1)}, u32[]{:S(2)}, u32[]{:S(2)}) collective-permute-start(bf16[64,2048]{1,0:T(8,128)(2,1)} %bitcast.6), channel_id=1, source_target_pairs={{0,1},{1,0},{2,3},{3,2},{4,5},{5,4},{6,7},{7,6},{8,9},{9,8},{10,11... | collective-permute-start | bytes 786440 | tf_op jit(solution)/shard_map/ppermute | solution.py:531
  9.4 1.9 %collective-permute-start.1 = (bf16[64,2048]{1,0:T(8,128)(2,1)}, bf16[64,2048]{1,0:T(8,128)(2,1)S(1)}, u32[]{:S(2)}, u32[]{:S(2)}) collective-permute-start(bf16[64,2048]{1,0:T(8,128)(2,1)} %bitcast.10), channel_id=1, source_target_pairs={{0,1},{1,0},{2,3},{3,2},{4,5},{5,4},{6,7},{7,6},{8,9},{9,8},{10,11... | collective-permute-start | bytes 786440 | tf_op jit(solution)/shard_map/ppermute | solution.py:532
  11.4 2.1 %steps.1 = (f32[16,40,128]{2,1,0:T(8,128)}, f32[8,128]{1,0:T(8,128)}) custom-call(f32[4,2048]{1,0:T(4,128)} %bitcast.14, f32[4]{0:T(128)} %alog_ref.5), custom_call_target="tpu_custom_call" | custom-call | flops 1000000 | bytes 100000 | tf_op jit(solution)/shard_map/steps/pallas_call | solution.py:504
  13.5 0.7 copy-done.3
  14.2 0.1 copy-done.4
  14.3 5.7 %ends.1 = (f32[32,8,384]{2,1,0:T(8,128)}, bf16[2048,256]{1,0:T(8,128)(2,1)}, bf16[2048,256]{1,0:T(8,128)(2,1)}, bf16[2048,256]{1,0:T(8,128)(2,1)}, bf16[2048,256...) custom-call(bf16[2048,256]{1,0:T(8,128)(2,1)} %x_ref.5, bf16[2048,256]{1,0:T(8,128)(2,1)} %dy_ref.5, ...), custom_call_target="tpu_custom_call" | custom-call | flops 1000000 | bytes 100000 | tf_op jit(solution)/shard_map/ends/pallas_call | solution.py:504
  20.0 7.5 %all-to-all-start = ((f32[32,8,384]{2,1,0:T(8,128)}), f32[32,8,384]{2,1,0:T(8,128)S(1)}, u32[]{:S(2)}, u32[]{:S(2)}) async-start(f32[32,8,384]{2,1,0:T(8,128)} %get-tuple-element.39.msg_ref), calls=%async_computation | async-start | bytes 786432 | tf_op jit(solution)/shard_map/all_to_all | solution.py:552
  27.5 7.2 %inner.1 = (f32[2048,256]{1,0:T(8,128)}, f32[128,2048]{1,0:T(8,128)}, f32[128,2048]{1,0:T(8,128)}, f32[16,8,128]{2,1,0:T(8,128)}) custom-call(bf16[2048,256]{1,0:T(8,128)(2,1)} %x_ref.5, bf16[2048,256]{1,0:T(8,128)(2,1)} %dy_ref.5, bf16[64,2048]{1,0:T(8,128)(2,1)} %bitcast.8, bf16[64,2048]{1,0:T(8,128)(2,1)} %copy-done.3, bf16[64,2048]{1,0:T(8,128)(2,1)} %bitcast.12, ...), custom_call_target="tpu_custom_call" | custom-call | flops 10000000000 | bytes 1000000000 | tf_op jit(solution)/shard_map/inner/pallas_call | solution.py:504
  34.8 6.5 %all-to-all-done.got_ref = f32[32,8,384]{2,1,0:T(8,128)S(1)} async-done(((f32[32,8,384]{2,1,0:T(8,128)}), f32[32,8,384]{2,1,0:T(8,128)S(1)}, u32[]{:S(2)}, u32[]{:S(2)}) %all-to-all-start) | async-done | bytes 393248 | tf_op jit(solution)/shard_map/all_to_all | solution.py:552
  41.3 0.8 copy-done
  42.1 1.8 %relay.1 = (f32[32,8,256]{2,1,0:T(8,128)}, f32[8,128]{1,0:T(8,128)}) custom-call(f32[32,8,384]{2,1,0:T(8,128)} %copy-done, f32[16,8,128]{2,1,0:T(8,128)} %get-tuple-element.41._.read_ref), custom_call_target="tpu_custom_call" | custom-call | flops 1000000 | bytes 100000 | tf_op jit(solution)/shard_map/relay/pallas_call | solution.py:504
  43.9 5.0 %all-to-all-start.1 = ((f32[32,8,256]{2,1,0:T(8,128)}), f32[32,8,256]{2,1,0:T(8,128)S(1)}, u32[]{:S(2)}, u32[]{:S(2)}) async-start(f32[32,8,256]{2,1,0:T(8,128)} %get-tuple-element.42), calls=%async_computation.1 | async-start | bytes 524288 | tf_op jit(solution)/shard_map/all_to_all | solution.py:564
  48.9 12.9 %states.1 = (f32[2048,256]{1,0:T(8,128)}, f32[128,2048]{1,0:T(8,128)}, f32[128,2048]{1,0:T(8,128)}, f32[16,8,128]{2,1,0:T(8,128)}, f32[2,128,256]{2,1,0:T(8,128)}, /*index=5*/f32[8,128]{1,0:T(8,128)}) custom-call(bf16[2048,256]{1,0:T(8,128)(2,1)} %x_ref.5, bf16[2048,256]{1,0:T(8,128)(2,1)} %dy_ref.5, bf16[64,2048]{1,0:T(8,128)(2,1)} %bitcast.9, ...), custom_call_target="tpu_custom_call" | custom-call | flops 10000000000 | bytes 1000000000 | tf_op jit(solution)/shard_map/states/pallas_call | solution.py:504
  61.8 0.7 copy-done.1
  62.5 2.1 %edge.1 = (bf16[2,128,256]{2,1,0:T(8,128)(2,1)}, bf16[2,128,256]{2,1,0:T(8,128)(2,1)}, f32[8,256]{1,0:T(8,128)}, f32[32,8,128]{2,1,0:T(8,128)}) custom-call(f32[32,8,256]{2,1,0:T(8,128)} %copy-done.1, f32[32,8,384]{2,1,0:T(8,128)} %get-tuple-element.39.msg_ref, f32[2,128,256]{2,1,0:T(8,128)} %get-tuple-element.51.slope_ref, ...), custom_call_target="tpu_custom_call" | custom-call | flops 1000000 | bytes 100000 | tf_op jit(solution)/shard_map/edge/pallas_call | solution.py:504
  64.6 5.7 %give.1 = (f32[128,2048]{1,0:T(8,128)}, f32[128,2048]{1,0:T(8,128)}) custom-call(bf16[2,128,256]{2,1,0:T(8,128)(2,1)} %get-tuple-element.53.start_ref, bf16[2,128,256]{2,1,0:T(8,128)(2,1)} %get-tuple-element.54.end_ref, bf16[2048,256]{1,0:T(8,128)(2,1)} %get-tuple-element.44.xd_ref.xh_ref, bf16[2048,256]{1,0:T(8,128)(2,1)} %get-tuple-element.45.xe_ref.xl_ref, ...), custom_call_target="tpu_custom_call" | custom-call | flops 1000000 | bytes 100000 | tf_op jit(solution)/shard_map/give/pallas_call | solution.py:504
  70.3 3.6 %collective-permute-start.2 = (f32[128,2048]{1,0:T(8,128)}, f32[128,2048]{1,0:T(8,128)S(1)}, u32[]{:S(2)}, u32[]{:S(2)}) collective-permute-start(f32[128,2048]{1,0:T(8,128)} %get-tuple-element.64), channel_id=1, source_target_pairs={{0,1},{1,0},{2,3},{3,2},{4,5},{5,4},{6,7},{7,6},{8,9},{9,8},{10,11... | collective-permute-start | bytes 3145736 | tf_op jit(solution)/shard_map/ppermute | solution.py:598
  73.9 9.5 %all-to-all-start.2 = ((f32[32,8,128]{2,1,0:T(8,128)}), f32[32,8,128]{2,1,0:T(8,128)S(1)}, u32[]{:S(2)}, u32[]{:S(2)}) async-start(f32[32,8,128]{2,1,0:T(8,128)} %get-tuple-element.60), calls=%async_computation.2 | async-start | bytes 262144 | tf_op jit(solution)/shard_map/all_to_all | solution.py:594
  83.4 0.6 slice_reduce_fusion.1
  84.1 6.5 %finish.1 = (bf16[2048,256]{1,0:T(8,128)(2,1)}, f32[4,2048]{1,0:T(4,128)}) custom-call(bf16[2,128,256]{2,1,0:T(8,128)(2,1)} %get-tuple-element.53.start_ref, bf16[2,128,256]{2,1,0:T(8,128)(2,1)} %get-tuple-element.54.end_ref, f32[8,256]{1,0:T(8,128)} %get-tuple-element.55.edge_ref, bf16[2048,256]{1,0:T(8,128)(2,1)} %get-tuple-element.44.xd_ref.xh_ref, ...), custom_call_target="tpu_custom_call" | custom-call | flops 1000000 | bytes 100000 | tf_op jit(solution)/shard_map/finish/pallas_call | solution.py:504
  90.5 2.9 %all-to-all-done.2 = f32[32,8,128]{2,1,0:T(8,128)S(1)} async-done(((f32[32,8,128]{2,1,0:T(8,128)}), f32[32,8,128]{2,1,0:T(8,128)S(1)}, u32[]{:S(2)}, u32[]{:S(2)}) %all-to-all-start.2) | async-done | bytes 131104 | tf_op jit(solution)/shard_map/all_to_all | solution.py:594
  93.4 0.7 slice_reduce_fusion
  94.1 1.0 %copy-done.2 = f32[128,2048]{1,0:T(8,128)} copy-done((f32[128,2048]{1,0:T(8,128)}, f32[128,2048]{1,0:T(8,128)S(1)}, u32[]{:S(2)}) %copy-start.2) | copy-done | bytes 1048600
  95.0 2.3 %join.1 = (bf16[64,2048]{1,0:T(8,128)(2,1)}, bf16[64,2048]{1,0:T(8,128)(2,1)}) custom-call(f32[128,2048]{1,0:T(8,128)} %get-tuple-element.63.keep_ref, f32[128,2048]{1,0:T(8,128)} %copy-done.2), custom_call_target="tpu_custom_call" | custom-call | flops 1000000 | bytes 100000 | tf_op jit(solution)/shard_map/join/pallas_call | solution.py:504
  (11 shorter events, 0.0 us)
Async XLA Ops:
  0.6 12.8 %collective-permute-start = (bf16[64,2048]{1,0:T(8,128)(2,1)}, bf16[64,2048]{1,0:T(8,128)(2,1)S(1)}, u32[]{:S(2)}, u32[]{:S(2)}) collective-permute-start(bf16[64,2048]{1,0:T(8,128)(2,1)} %bitcast.6), channel_id=1, source_target_pairs={{0,1},{1,0},{2,3},{3,2},{4,5},{5,4},{6,7},{7,6},{8,9},{9,8},{10,11... | collective-permute-start | bytes 786440 | tf_op jit(solution)/shard_map/ppermute | solution.py:531
  9.4 4.0 %collective-permute-start.1 = (bf16[64,2048]{1,0:T(8,128)(2,1)}, bf16[64,2048]{1,0:T(8,128)(2,1)S(1)}, u32[]{:S(2)}, u32[]{:S(2)}) collective-permute-start(bf16[64,2048]{1,0:T(8,128)(2,1)} %bitcast.10), channel_id=1, source_target_pairs={{0,1},{1,0},{2,3},{3,2},{4,5},{5,4},{6,7},{7,6},{8,9},{9,8},{10,11... | collective-permute-start | bytes 786440 | tf_op jit(solution)/shard_map/ppermute | solution.py:532
  13.5 0.7 copy-start.3
  13.5 0.8 copy-start.4
  20.0 21.3 %all-to-all-start = ((f32[32,8,384]{2,1,0:T(8,128)}), f32[32,8,384]{2,1,0:T(8,128)S(1)}, u32[]{:S(2)}, u32[]{:S(2)}) async-start(f32[32,8,384]{2,1,0:T(8,128)} %get-tuple-element.39.msg_ref), calls=%async_computation | async-start | bytes 786432 | tf_op jit(solution)/shard_map/all_to_all | solution.py:552
  41.3 0.8 copy-start
  43.9 17.9 %all-to-all-start.1 = ((f32[32,8,256]{2,1,0:T(8,128)}), f32[32,8,256]{2,1,0:T(8,128)S(1)}, u32[]{:S(2)}, u32[]{:S(2)}) async-start(f32[32,8,256]{2,1,0:T(8,128)} %get-tuple-element.42), calls=%async_computation.1 | async-start | bytes 524288 | tf_op jit(solution)/shard_map/all_to_all | solution.py:564
  61.8 0.7 copy-start.1
  64.6 18.9 %copy-start.5 = (f32[8,128]{1,0:T(8,128)S(1)}, f32[8,128]{1,0:T(8,128)}, u32[]{:S(2)}) copy-start(f32[8,128]{1,0:T(8,128)} %get-tuple-element.67) | copy-start | bytes 12292
  70.3 23.8 %collective-permute-start.2 = (f32[128,2048]{1,0:T(8,128)}, f32[128,2048]{1,0:T(8,128)S(1)}, u32[]{:S(2)}, u32[]{:S(2)}) collective-permute-start(f32[128,2048]{1,0:T(8,128)} %get-tuple-element.64), channel_id=1, source_target_pairs={{0,1},{1,0},{2,3},{3,2},{4,5},{5,4},{6,7},{7,6},{8,9},{9,8},{10,11... | collective-permute-start | bytes 3145736 | tf_op jit(solution)/shard_map/ppermute | solution.py:598
  73.9 19.5 %all-to-all-start.2 = ((f32[32,8,128]{2,1,0:T(8,128)}), f32[32,8,128]{2,1,0:T(8,128)S(1)}, u32[]{:S(2)}, u32[]{:S(2)}) async-start(f32[32,8,128]{2,1,0:T(8,128)} %get-tuple-element.60), calls=%async_computation.2 | async-start | bytes 262144 | tf_op jit(solution)/shard_map/all_to_all | solution.py:594
  94.1 1.0 %copy-start.2 = (f32[128,2048]{1,0:T(8,128)}, f32[128,2048]{1,0:T(8,128)S(1)}, u32[]{:S(2)}) copy-start(f32[128,2048]{1,0:T(8,128)S(1)} %collective-permute-done.2.back_ref) | copy-start | bytes 3145732

commit v2 on v1

--- a/solution.py
+++ b/solution.py
@@ -425,8 +425,9 @@
 
 def finish_kernel(
     heads, width, start_ref, end_ref, edge_ref, xh_ref, xl_ref, yh_ref, yl_ref, b_ref, c_ref, tab_ref, rows_ref, dt_ref,
-    alog_ref, gxl_ref, gx_ref, gdt_ref, diffs,
+    alog_ref, gxl_ref, gbl_ref, gcl_ref, gx_ref, gdt_ref, keep_ref, give_ref, diffs,
 ):
+    give_kernel(start_ref, end_ref, xh_ref, xl_ref, yh_ref, yl_ref, gbl_ref, gcl_ref, keep_ref, give_ref)
     turn, last = pl.program_id(0), pl.num_programs(0) - 1
     full = heads * width
     blocks = tab_ref.shape[0]
@@ -592,19 +593,17 @@
         [(pair, "w"), (pair, "w"), (shape((8, full), F32), "w"), (shape((ring, 8, T), F32), "w")],
     )(carry, msg, slopes, loga, tab)
     loga_all = lax.all_to_all(sums, "ctx", 0, 0, tiled=True)
-    keep, give = call(
-        give_kernel, "give", n, ["w", "w", rows, rows, rows, rows, cols, cols], [(long, cols)] * 2, flops=10**6
-    )(start, end, xh, xl, yh, yl, gbl, gcl)
-    back = lax.ppermute(give, "exp", pairs)
-    gx, gdt = call(
+    gx, gdt, keep, give = call(
         part(finish_kernel, heads, width),
         "finish",
         n,
-        ["w", "w", "w"] + [rows] * 6 + ["w", "w", "w", "s", rows],
-        [(wide, rows), (shape((heads, tokens), F32), "w")],
+        ["w", "w", "w"] + [rows] * 6 + ["w", "w", "w", "s", rows, cols, cols],
+        [(wide, rows), (shape((heads, tokens), F32), "w"), (long, cols), (long, cols)],
         [pltpu.VMEM((blocks, 2 * heads, T), F32)],
-        flops=10**6,
-    )(start, end, edge, xh, xl, yh, yl, bt, ct, tab, rate, dt, a_log, gxl)
+        flops=10**10,
+    )(start, end, edge, xh, xl, yh, yl, bt, ct, tab, rate, dt, a_log, gxl, gbl, gcl)
+    give, loga_all = lax.optimization_barrier((give, loga_all))
+    back = lax.ppermute(give, "exp", pairs)
     out = shape((half, tokens), BF16)
     gb, gc = call(join_kernel, "join", n, [cols, cols], [(out, cols)] * 2)(keep, back)
     grad_skip = jnp.sum(skip[0:heads], axis=1)

time: 97.9 us -> 94.7 us (0.967)
  Pallas kernels: 46.3 us -> 43.2 us
  waiting for transfers between devices: 9.4 us -> 7.99 us
  starting transfers between devices: 36.4 us -> 37.8 us
    pallas_call x9 -> x8, Pallas kernels: 46.3 us -> 43.2 us  [run(): pl.pallas_call(kernel, name=name, grid=(turns,), out_shape=tuple((shape f...]
    all_to_all x1, waiting for transfers between devices: 2.85 us -> 0.18 us  [per_device(): loga_all = lax.all_to_all(sums, 'ctx', 0, 0, tiled=True)]
    ppermute x1, starting transfers between devices: 3.61 us -> 5.26 us  [per_device(): back = lax.ppermute(give, 'exp', pairs)]
    ppermute x1, waiting for transfers between devices: 0.01 us -> 1.19 us  [per_device(): back = lax.ppermute(give, 'exp', pairs)]
  transfers between devices with their start and end apart: 6 -> 6, of which waited for: 2 -> 3; matrix products, arithmetic and copies ran while one was open for 1% -> 1% of each run, Pallas kernels for 29% -> 33%
where the time goes in v2:
time: 94.7 us; the launch traced here: 94.2 us
  Pallas kernels  43.2 us (46%)
  starting transfers between devices  37.8 us (40%)
  waiting for transfers between devices  7.99 us (8%)
  local copies, waits for them, and re-layouts  3.21 us (3%)
  other arithmetic  1.28 us (1%)
    pallas_call x8, Pallas kernels, run(): pl.pallas_call(kernel, name=name, grid=(turns,), out_shape=tuple((shape f...  43.2 us
    all_to_all x1, starting transfers between devices, per_device(): loga_all = lax.all_to_all(sums, 'ctx', 0, 0, tiled=True)  9.22 us
    ppermute x1, starting transfers between devices, per_device(): pb = lax.ppermute(b, 'exp', pairs)  8.79 us
    all_to_all x1, starting transfers between devices, per_device(): got = lax.all_to_all(msg, 'ctx', 0, 0, tiled=True)  7.53 us
    all_to_all x1, waiting for transfers between devices, per_device(): got = lax.all_to_all(msg, 'ctx', 0, 0, tiled=True)  6.62 us
    ppermute x1, starting transfers between devices, per_device(): back = lax.ppermute(give, 'exp', pairs)  5.26 us
    all_to_all x1, starting transfers between devices, per_device(): carry = lax.all_to_all(sent, 'ctx', 0, 0, tiled=True)  5.03 us
    unnamed x12, local copies, waits for them, and re-layouts  3.21 us
  transfers between devices with their start and end apart: 6, of which 3 were waited for; matrix products, arithmetic and copies ran while one was open for 1% of the time, Pallas kernels for 33%

profile of v2, /device:TPU:1, one launch (start us, length us, event | category | flops | bytes accessed | tf_op | source)
XLA Modules:
  0.0 94.2 jit_solution(8764410219861663933)
XLA Ops:
  0.6 8.8 %collective-permute-start = (bf16[64,2048]{1,0:T(8,128)(2,1)}, bf16[64,2048]{1,0:T(8,128)(2,1)S(1)}, u32[]{:S(2)}, u32[]{:S(2)}) collective-permute-start(bf16[64,2048]{1,0:T(8,128)(2,1)} %bitcast.6), channel_id=1, source_target_pairs={{0,1},{1,0},{2,3},{3,2},{4,5},{5,4},{6,7},{7,6},{8,9},{9,8},{10,11... | collective-permute-start | bytes 786440 | tf_op jit(solution)/shard_map/ppermute | solution.py:532
  9.4 1.9 %collective-permute-start.1 = (bf16[64,2048]{1,0:T(8,128)(2,1)}, bf16[64,2048]{1,0:T(8,128)(2,1)S(1)}, u32[]{:S(2)}, u32[]{:S(2)}) collective-permute-start(bf16[64,2048]{1,0:T(8,128)(2,1)} %bitcast.10), channel_id=1, source_target_pairs={{0,1},{1,0},{2,3},{3,2},{4,5},{5,4},{6,7},{7,6},{8,9},{9,8},{10,11... | collective-permute-start | bytes 786440 | tf_op jit(solution)/shard_map/ppermute | solution.py:533
  11.4 2.1 %steps.1 = (f32[16,40,128]{2,1,0:T(8,128)}, f32[8,128]{1,0:T(8,128)}) custom-call(f32[4,2048]{1,0:T(4,128)} %bitcast.14, f32[4]{0:T(128)} %alog_ref.5), custom_call_target="tpu_custom_call" | custom-call | flops 1000000 | bytes 100000 | tf_op jit(solution)/shard_map/steps/pallas_call | solution.py:505
  13.5 0.7 copy-done.3
  14.2 0.1 copy-done.4
  14.2 5.7 %ends.1 = (f32[32,8,384]{2,1,0:T(8,128)}, bf16[2048,256]{1,0:T(8,128)(2,1)}, bf16[2048,256]{1,0:T(8,128)(2,1)}, bf16[2048,256]{1,0:T(8,128)(2,1)}, bf16[2048,256...) custom-call(bf16[2048,256]{1,0:T(8,128)(2,1)} %x_ref.5, bf16[2048,256]{1,0:T(8,128)(2,1)} %dy_ref.5, ...), custom_call_target="tpu_custom_call" | custom-call | flops 1000000 | bytes 100000 | tf_op jit(solution)/shard_map/ends/pallas_call | solution.py:505
  20.0 7.5 %all-to-all-start = ((f32[32,8,384]{2,1,0:T(8,128)}), f32[32,8,384]{2,1,0:T(8,128)S(1)}, u32[]{:S(2)}, u32[]{:S(2)}) async-start(f32[32,8,384]{2,1,0:T(8,128)} %get-tuple-element.41.msg_ref), calls=%async_computation | async-start | bytes 786432 | tf_op jit(solution)/shard_map/all_to_all | solution.py:553
  27.5 7.2 %inner.1 = (f32[2048,256]{1,0:T(8,128)}, f32[128,2048]{1,0:T(8,128)}, f32[128,2048]{1,0:T(8,128)}, f32[16,8,128]{2,1,0:T(8,128)}) custom-call(bf16[2048,256]{1,0:T(8,128)(2,1)} %x_ref.5, bf16[2048,256]{1,0:T(8,128)(2,1)} %dy_ref.5, bf16[64,2048]{1,0:T(8,128)(2,1)} %bitcast.8, bf16[64,2048]{1,0:T(8,128)(2,1)} %copy-done.3, bf16[64,2048]{1,0:T(8,128)(2,1)} %bitcast.12, ...), custom_call_target="tpu_custom_call" | custom-call | flops 10000000000 | bytes 1000000000 | tf_op jit(solution)/shard_map/inner/pallas_call | solution.py:505
  34.7 6.6 %all-to-all-done.got_ref = f32[32,8,384]{2,1,0:T(8,128)S(1)} async-done(((f32[32,8,384]{2,1,0:T(8,128)}), f32[32,8,384]{2,1,0:T(8,128)S(1)}, u32[]{:S(2)}, u32[]{:S(2)}) %all-to-all-start) | async-done | bytes 393248 | tf_op jit(solution)/shard_map/all_to_all | solution.py:553
  41.3 0.8 copy-done
  42.0 1.8 %relay.1 = (f32[32,8,256]{2,1,0:T(8,128)}, f32[8,128]{1,0:T(8,128)}) custom-call(f32[32,8,384]{2,1,0:T(8,128)} %copy-done, f32[16,8,128]{2,1,0:T(8,128)} %get-tuple-element.43._.read_ref), custom_call_target="tpu_custom_call" | custom-call | flops 1000000 | bytes 100000 | tf_op jit(solution)/shard_map/relay/pallas_call | solution.py:505
  43.8 5.0 %all-to-all-start.1 = ((f32[32,8,256]{2,1,0:T(8,128)}), f32[32,8,256]{2,1,0:T(8,128)S(1)}, u32[]{:S(2)}, u32[]{:S(2)}) async-start(f32[32,8,256]{2,1,0:T(8,128)} %get-tuple-element.44), calls=%async_computation.1 | async-start | bytes 524288 | tf_op jit(solution)/shard_map/all_to_all | solution.py:565
  48.9 12.8 %states.1 = (f32[2048,256]{1,0:T(8,128)}, f32[128,2048]{1,0:T(8,128)}, f32[128,2048]{1,0:T(8,128)}, f32[16,8,128]{2,1,0:T(8,128)}, f32[2,128,256]{2,1,0:T(8,128)}, /*index=5*/f32[8,128]{1,0:T(8,128)}) custom-call(bf16[2048,256]{1,0:T(8,128)(2,1)} %x_ref.5, bf16[2048,256]{1,0:T(8,128)(2,1)} %dy_ref.5, bf16[64,2048]{1,0:T(8,128)(2,1)} %bitcast.9, ...), custom_call_target="tpu_custom_call" | custom-call | flops 10000000000 | bytes 1000000000 | tf_op jit(solution)/shard_map/states/pallas_call | solution.py:505
  61.7 0.7 copy-done.1
  62.4 2.1 %edge.1 = (bf16[2,128,256]{2,1,0:T(8,128)(2,1)}, bf16[2,128,256]{2,1,0:T(8,128)(2,1)}, f32[8,256]{1,0:T(8,128)}, f32[32,8,128]{2,1,0:T(8,128)}) custom-call(f32[32,8,256]{2,1,0:T(8,128)} %copy-done.1, f32[32,8,384]{2,1,0:T(8,128)} %get-tuple-element.41.msg_ref, f32[2,128,256]{2,1,0:T(8,128)} %get-tuple-element.53.slope_ref, ...), custom_call_target="tpu_custom_call" | custom-call | flops 1000000 | bytes 100000 | tf_op jit(solution)/shard_map/edge/pallas_call | solution.py:505
  64.5 9.2 %all-to-all-start.2 = ((f32[32,8,128]{2,1,0:T(8,128)}), f32[32,8,128]{2,1,0:T(8,128)S(1)}, u32[]{:S(2)}, u32[]{:S(2)}) async-start(f32[32,8,128]{2,1,0:T(8,128)} %get-tuple-element.65), calls=%async_computation.2 | async-start | bytes 262144 | tf_op jit(solution)/shard_map/all_to_all | solution.py:595
  73.7 9.3 %finish.1 = (bf16[2048,256]{1,0:T(8,128)(2,1)}, f32[4,2048]{1,0:T(4,128)}, f32[128,2048]{1,0:T(8,128)}, f32[128,2048]{1,0:T(8,128)}) custom-call(bf16[2,128,256]{2,1,0:T(8,128)(2,1)} %get-tuple-element.55.start_ref, bf16[2,128,256]{2,1,0:T(8,128)(2,1)} %get-tuple-element.56.end_ref, f32[8,256]{1,0:T(8,128)} %get-tuple-element.57.edge_ref, ...), custom_call_target="tpu_custom_call" | custom-call | flops 10000000000 | bytes 1000000000 | tf_op jit(solution)/shard_map/finish/pallas_call | solution.py:505
  83.0 0.2 all-to-all-done.2
  83.2 5.3 %collective-permute-start.2 = (f32[128,2048]{1,0:T(8,128)}, f32[128,2048]{1,0:T(8,128)S(1)}, u32[]{:S(2)}, u32[]{:S(2)}) collective-permute-start(f32[128,2048]{1,0:T(8,128)} %get-tuple-element.68), channel_id=1, source_target_pairs={{0,1},{1,0},{2,3},{3,2},{4,5},{5,4},{6,7},{7,6},{8,9},{9,8},{10,11... | collective-permute-start | bytes 3145736 | tf_op jit(solution)/shard_map/ppermute | solution.py:606
  88.4 0.6 slice_reduce_fusion.1
  89.1 0.7 slice_reduce_fusion
  89.7 1.2 %collective-permute-done.2.back_ref = f32[128,2048]{1,0:T(8,128)S(1)} collective-permute-done((f32[128,2048]{1,0:T(8,128)}, f32[128,2048]{1,0:T(8,128)S(1)}, u32[]{:S(2)}, u32[]{:S(2)}) %collective-permute-start.2) | collective-permute-done | bytes 1048608 | tf_op jit(solution)/shard_map/ppermute | solution.py:606
  90.9 1.0 %copy-done.2 = f32[128,2048]{1,0:T(8,128)} copy-done((f32[128,2048]{1,0:T(8,128)}, f32[128,2048]{1,0:T(8,128)S(1)}, u32[]{:S(2)}) %copy-start.2) | copy-done | bytes 1048600
  91.9 2.3 %join.1 = (bf16[64,2048]{1,0:T(8,128)(2,1)}, bf16[64,2048]{1,0:T(8,128)(2,1)}) custom-call(f32[128,2048]{1,0:T(8,128)} %get-tuple-element.67.keep_ref, f32[128,2048]{1,0:T(8,128)} %copy-done.2), custom_call_target="tpu_custom_call" | custom-call | flops 1000000 | bytes 100000 | tf_op jit(solution)/shard_map/join/pallas_call | solution.py:505
  (10 shorter events, 0.0 us)
Async XLA Ops:
  0.6 12.8 %collective-permute-start = (bf16[64,2048]{1,0:T(8,128)(2,1)}, bf16[64,2048]{1,0:T(8,128)(2,1)S(1)}, u32[]{:S(2)}, u32[]{:S(2)}) collective-permute-start(bf16[64,2048]{1,0:T(8,128)(2,1)} %bitcast.6), channel_id=1, source_target_pairs={{0,1},{1,0},{2,3},{3,2},{4,5},{5,4},{6,7},{7,6},{8,9},{9,8},{10,11... | collective-permute-start | bytes 786440 | tf_op jit(solution)/shard_map/ppermute | solution.py:532
  9.4 4.0 %collective-permute-start.1 = (bf16[64,2048]{1,0:T(8,128)(2,1)}, bf16[64,2048]{1,0:T(8,128)(2,1)S(1)}, u32[]{:S(2)}, u32[]{:S(2)}) collective-permute-start(bf16[64,2048]{1,0:T(8,128)(2,1)} %bitcast.10), channel_id=1, source_target_pairs={{0,1},{1,0},{2,3},{3,2},{4,5},{5,4},{6,7},{7,6},{8,9},{9,8},{10,11... | collective-permute-start | bytes 786440 | tf_op jit(solution)/shard_map/ppermute | solution.py:533
  13.5 0.7 copy-start.3
  13.5 0.8 copy-start.4
  20.0 21.3 %all-to-all-start = ((f32[32,8,384]{2,1,0:T(8,128)}), f32[32,8,384]{2,1,0:T(8,128)S(1)}, u32[]{:S(2)}, u32[]{:S(2)}) async-start(f32[32,8,384]{2,1,0:T(8,128)} %get-tuple-element.41.msg_ref), calls=%async_computation | async-start | bytes 786432 | tf_op jit(solution)/shard_map/all_to_all | solution.py:553
  41.3 0.8 copy-start
  43.8 17.9 %all-to-all-start.1 = ((f32[32,8,256]{2,1,0:T(8,128)}), f32[32,8,256]{2,1,0:T(8,128)S(1)}, u32[]{:S(2)}, u32[]{:S(2)}) async-start(f32[32,8,256]{2,1,0:T(8,128)} %get-tuple-element.44), calls=%async_computation.1 | async-start | bytes 524288 | tf_op jit(solution)/shard_map/all_to_all | solution.py:565
  61.7 0.7 copy-start.1
  64.5 18.7 %all-to-all-start.2 = ((f32[32,8,128]{2,1,0:T(8,128)}), f32[32,8,128]{2,1,0:T(8,128)S(1)}, u32[]{:S(2)}, u32[]{:S(2)}) async-start(f32[32,8,128]{2,1,0:T(8,128)} %get-tuple-element.65), calls=%async_computation.2 | async-start | bytes 262144 | tf_op jit(solution)/shard_map/all_to_all | solution.py:595
  73.7 14.7 %copy-start.5 = (f32[8,128]{1,0:T(8,128)S(1)}, f32[8,128]{1,0:T(8,128)}, u32[]{:S(2)}) copy-start(f32[8,128]{1,0:T(8,128)} %get-tuple-element.71) | copy-start | bytes 12292
  83.2 7.7 %collective-permute-start.2 = (f32[128,2048]{1,0:T(8,128)}, f32[128,2048]{1,0:T(8,128)S(1)}, u32[]{:S(2)}, u32[]{:S(2)}) collective-permute-start(f32[128,2048]{1,0:T(8,128)} %get-tuple-element.68), channel_id=1, source_target_pairs={{0,1},{1,0},{2,3},{3,2},{4,5},{5,4},{6,7},{7,6},{8,9},{9,8},{10,11... | collective-permute-start | bytes 3145736 | tf_op jit(solution)/shard_map/ppermute | solution.py:606
  90.9 1.0 %copy-start.2 = (f32[128,2048]{1,0:T(8,128)}, f32[128,2048]{1,0:T(8,128)S(1)}, u32[]{:S(2)}) copy-start(f32[128,2048]{1,0:T(8,128)S(1)} %collective-permute-done.2.back_ref) | copy-start | bytes 3145732
